TPU v7x, 128 devices: a whole 4x4x4 slice. The times are simulated.
128 devices in a mesh: ep: 32 (over y, z, core), tp: 4 (over x).
Axes of the slice: x: 4, y: 4, z: 4, core: 2. Of those that a mesh axis runs over, the one named last changes fastest.
Arguments:
- residual: bfloat16 [4096, 4096], P('ep'), may hold values from -5 to 5
- queries: bfloat16 [4096, 4096], P('ep', 'tp'), may hold values from -120 to 120
- new_keys: bfloat16 [4096, 512], P('ep', 'tp'), may hold values from -4 to 4
- new_values: bfloat16 [4096, 512], P('ep', 'tp'), may hold values from -4 to 4
- cache_keys: bfloat16 [128, 1024, 512], P('ep', None, 'tp'), may hold values from -4 to 4
- cache_values: bfloat16 [128, 1024, 512], P('ep', None, 'tp'), may hold values from -4 to 4
- new_count: int32 [128], P('ep'), may hold values from 2 to 64, as said below
- cached_len: int32 [128], P('ep'), may hold values from 128 to 1024, as said below
- out_proj: bfloat16 [4096, 4096], P('tp'), may hold values from -0.75 to 0.75
- norm_gain: bfloat16 [4096], replicated, may hold values from 0.099609375 to 1.8984375
- expert_ids: int32 [4096, 8], P('ep'), may hold values from 0 to 63, all different within a row; in each aligned block of 128 rows (0 to 127, 128 to 255, ...) at most 32 rows name the same one
- gate_scale: float32 [4096, 8], P('ep'), may hold values from 0.02 to 0.3
- w_gate: bfloat16 [64, 4096, 768], P('ep', None, 'tp'), may hold values from -0.09375 to 0.09375
- w_up: bfloat16 [64, 4096, 768], P('ep', None, 'tp'), may hold values from -0.09375 to 0.09375
- w_down: bfloat16 [64, 768, 4096], P('ep', 'tp'), may hold values from -0.21875 to 0.21875
Outputs:
- layer_out: bfloat16 [4096, 4096], P('ep', 'tp')
Inputs may be any that keep to these rules, and one draw needn't show every extreme that they name: `new_count`: each count is even; the counts of a group's 4 conversations sum to 128, and one of them is 64. `cached_len`: in every group one conversation has 1024. `expert_ids`: 8 different experts a token; among the 128 tokens of one group no expert is named more than 32 times.
All inputs are finite; a program needn't handle non-finite values.
Results may differ from a plain program's by a relative error of at most 0.02.
Values may be sent and summed in bfloat16 or wider, within the bound.
No kernel may reach another device: no remote copies, remote signals or barrier semaphores. Data moves between devices by JAX's collectives and lax.ppermute only.
A program may use at most 128 MiB of HBM per device.

v0:
```python
import jax
import jax.numpy as jnp
from jax import lax
from jax.sharding import PartitionSpec as P

D = 4096
HD = 128


norm_eps = 1e-06
neg_fill = -1e30


def attend(queries, new_keys, new_values, cache_keys, cache_values, new_count, cached_len):
    tokens = queries.shape[0]
    kv_count = new_keys.shape[1] // HD
    per_head = queries.shape[1] // HD // kv_count
    convs = cache_keys.shape[0]
    depth = cache_keys.shape[1]
    position = jnp.arange(tokens, dtype=jnp.int32)
    run_ends = jnp.cumsum(new_count)
    conv_of = jnp.sum((position[:, None] >= run_ends[None, :]).astype(jnp.int32), axis=1)
    cache_ok = (conv_of[:, None, None] == jnp.arange(convs, dtype=jnp.int32)[None, :, None]) & (
        jnp.arange(depth, dtype=jnp.int32)[None, None, :] < cached_len[None, :, None]
    )
    cache_ok = cache_ok.reshape(tokens, convs * depth)
    new_ok = (conv_of[:, None] == conv_of[None, :]) & (position[None, :] <= position[:, None])
    query_heads = queries.reshape(tokens, kv_count, per_head, HD)
    keys_cached = cache_keys.reshape(convs * depth, kv_count, HD)
    values_cached = cache_values.reshape(convs * depth, kv_count, HD)
    keys_fresh = new_keys.reshape(tokens, kv_count, HD)
    values_fresh = new_values.reshape(tokens, kv_count, HD)
    inv_root = HD ** (-0.5)
    cache_score = (
        jnp.einsum("tkgd,nkd->tkgn", query_heads, keys_cached, preferred_element_type=jnp.float32)
        * inv_root
    )
    fresh_score = (
        jnp.einsum("tkgd,skd->tkgs", query_heads, keys_fresh, preferred_element_type=jnp.float32)
        * inv_root
    )
    cache_score = jnp.where(cache_ok[:, None, None, :], cache_score, neg_fill)
    fresh_score = jnp.where(new_ok[:, None, None, :], fresh_score, neg_fill)
    top_score = jnp.maximum(jnp.max(cache_score, axis=-1), jnp.max(fresh_score, axis=-1))[..., None]
    cache_exp = jnp.exp(cache_score - top_score)
    fresh_exp = jnp.exp(fresh_score - top_score)
    denom_sum = jnp.sum(cache_exp, axis=-1, keepdims=True) + jnp.sum(
        fresh_exp, axis=-1, keepdims=True
    )
    cache_wts = (cache_exp / denom_sum).astype(jnp.bfloat16)
    fresh_wts = (fresh_exp / denom_sum).astype(jnp.bfloat16)
    attended = jnp.einsum(
        "tkgn,nkd->tkgd", cache_wts, values_cached, preferred_element_type=jnp.float32
    )
    attended = attended + jnp.einsum(
        "tkgs,skd->tkgd", fresh_wts, values_fresh, preferred_element_type=jnp.float32
    )
    return attended.astype(jnp.bfloat16).reshape(tokens, kv_count * per_head * HD)


def on_device(
    residual,
    queries,
    new_keys,
    new_values,
    cache_keys,
    cache_values,
    new_count,
    cached_len,
    out_proj,
    norm_gain,
    expert_ids,
    gate_scale,
    w_gate,
    w_up,
    w_down,
):
    tokens = residual.shape[0]
    attended = attend(
        queries, new_keys, new_values, cache_keys, cache_values, new_count, cached_len
    )
    partial_proj = jnp.dot(attended, out_proj, preferred_element_type=jnp.float32)
    quarter = D // lax.axis_size("tp")
    offset = lax.axis_index("tp") * quarter
    projected = lax.psum(partial_proj.astype(jnp.bfloat16), "tp").astype(jnp.float32)
    stream = (residual.astype(jnp.float32) + projected).astype(jnp.bfloat16)
    stream_f = stream.astype(jnp.float32)
    mean_square = jnp.mean(stream_f * stream_f, axis=-1, keepdims=True)
    normed = (stream_f * lax.rsqrt(mean_square + norm_eps) * norm_gain.astype(jnp.float32)).astype(
        jnp.bfloat16
    )
    own_cols = lax.dynamic_slice_in_dim(stream, offset, quarter, 1)
    experts = w_gate.shape[0] * lax.axis_size("ep")
    topk = expert_ids.shape[1]
    capacity = 2 * tokens * topk // experts
    flat_ids = expert_ids.reshape(-1)
    onehot = (flat_ids[:, None] == jnp.arange(experts, dtype=jnp.int32)[None, :]).astype(jnp.int32)
    slot_of = jnp.sum((jnp.cumsum(onehot, axis=0) - onehot) * onehot, axis=1)
    target = flat_ids * capacity + slot_of
    token_of = jnp.arange(tokens * topk, dtype=jnp.int32) // topk
    outgoing = (
        jnp.zeros((experts * capacity, normed.shape[1]), jnp.bfloat16)
        .at[target]
        .set(normed[token_of])
    )
    outgoing = outgoing.reshape(experts, capacity, normed.shape[1])
    arrived = lax.all_to_all(outgoing, "ep", split_axis=0, concat_axis=0, tiled=True)
    sources = lax.axis_size("ep")
    local_count = w_gate.shape[0]
    items = arrived.shape[1]
    rows_in = arrived.reshape(sources, local_count, items, arrived.shape[2])
    gate_part = jnp.einsum("secd,edf->secf", rows_in, w_gate, preferred_element_type=jnp.float32)
    up_part = jnp.einsum("secd,edf->secf", rows_in, w_up, preferred_element_type=jnp.float32)
    activated = (jax.nn.silu(gate_part) * up_part).astype(jnp.bfloat16)
    down_part = jnp.einsum("secf,efd->secd", activated, w_down, preferred_element_type=jnp.float32)
    summed = lax.psum_scatter(down_part.astype(jnp.bfloat16), "tp", scatter_dimension=3, tiled=True)
    summed = summed.reshape(sources * local_count, items, summed.shape[3])
    returned = lax.all_to_all(summed, "ep", split_axis=0, concat_axis=0, tiled=True)
    picked = returned.reshape(experts * capacity, quarter)[target].reshape(tokens, topk, quarter)
    mixture = jnp.sum(picked.astype(jnp.float32) * gate_scale[:, :, None], axis=1)
    return (own_cols.astype(jnp.float32) + mixture).astype(jnp.bfloat16)


def solution(mesh):
    in_specs = (
        P("ep", None),
        P("ep", "tp"),
        P("ep", "tp"),
        P("ep", "tp"),
        P("ep", None, "tp"),
        P("ep", None, "tp"),
        P("ep"),
        P("ep"),
        P("tp", None),
        P(),
        P("ep", None),
        P("ep", None),
        P("ep", None, "tp"),
        P("ep", None, "tp"),
        P("ep", "tp", None),
    )
    out_specs = P("ep", "tp")
    return jax.shard_map(
        on_device, mesh=mesh, in_specs=in_specs, out_specs=out_specs, check_vma=False
    )
```

profile of v0, /device:TPU:32, one launch (start us, length us, event | category | flops | bytes accessed | tf_op | source)
XLA Modules:
  0.0 594.4 jit_solution(16764052489525172998)
XLA Ops:
  6.5 1.0 reduce-window.18
  7.5 0.1 convert_reduce_fusion
  7.6 0.1 fusion.40
  7.7 0.7 lt.48
  8.5 0.7 bitcast_and_fusion
  9.2 0.0 copy-start.4
  9.2 0.0 copy-start.5
  9.2 9.7 %fusion.5 = (f32[128,8]{0,1:T(8,128)S(1)}, f32[4096,128,8]{1,0,2:T(8,128)}) fusion(pred[128,4096]{0,1:T(8,128)(4,1)S(1)} %bitcast_and_fusion, bf16[4096,128,1]{1,0,2:T(8,128)(2,1)} %bitcast.145, bf16[128,1024]{1,0:T(8,128)(2,1)} %param.16), kind=kOutput, calls=%fused_computation.12 | convolution fusion | flops 1086323712 | bytes 18616320 | tf_op jit(solution)/shard_map/tkgd,nkd->tkgn/dot_general | solution.py:35
  18.9 1.0 fusion.45
  19.9 9.2 %fusion = f32[128,8]{0,1:T(8,128)S(1)} fusion(f32[4096,128,8]{1,0,2:T(8,128)} %get-tuple-element.8, f32[128,8]{0,1:T(8,128)S(1)} %max.9, pred[128,4096]{0,1:T(8,128)(4,1)} %copy-done.1), kind=kLoop, calls=%fused_computation.7 | loop fusion | flops 16776192 | bytes 17309696 | tf_op jit(solution)/shard_map/reduce_sum | solution.py:47
  29.1 1.1 fusion.28
  30.3 0.0 copy-start.9
  30.3 8.5 %fusion.6 = f32[128,8,128]{0,2,1:T(8,128)S(1)} fusion(bf16[4096,128,1]{1,0,2:T(8,128)(2,1)} %bitcast.153, f32[4096,128,8]{1,0,2:T(8,128)} %get-tuple-element.8, f32[128,8]{0,1:T(8,128)S(1)} %add.84, f32[128,8]{0,1:T(8,128)S(1)} %max.9, pred[128,4096]{0,1:T(8,128)(4,1)} %copy-done.1), kind=kOutput, calls=%fused_computation.13 | convolution fusion | flops 1094713344 | bytes 18882560 | tf_op jit(solution)/shard_map/tkgn,nkd->tkgd/dot_general | solution.py:52
  38.9 0.3 fusion.26
  39.1 5.7 convolution_convert_fusion
  44.9 0.0 all-reduce.2.cloned.1.call-update
  44.9 0.6 reduce-scatter.2.cloned.1.call-start
  45.5 0.1 copy.44
  45.6 0.1 eq.70
  45.7 0.1 eq.66
  45.8 0.7 fusion.37
  46.5 31.1 %reduce-window.19 = s32[64,8,128]{2,1,0:T(8,128)S(1)} reduce-window(s32[64,8,128]{2,1,0:T(8,128)} %fusion.37, s32[]{:T(128)} %constant.18.clone.1), window={size=1x1x128 pad=0_0x0_0x127_0}, to_apply=%region_7.8 | reduce-window | flops 8323072 | bytes 524292 | tf_op jit(solution)/shard_map/reduce-window.1
  77.6 0.8 slice.12
  78.4 1.1 copy.46
  79.6 0.1 copy.47
  79.7 0.1 copy.43
  79.8 0.1 mul.91
  79.9 0.1 broadcast_add_fusion
  80.0 0.1 fusion.31
  80.1 12.8 %all-reduce.2.cloned.1.call-done = bf16[128,4096]{1,0:T(8,128)(2,1)} async-done(((bf16[128,4096]{1,0:T(8,128)(2,1)}), bf16[128,4096]{1,0:T(8,128)(2,1)}) %all-reduce.2.cloned.1.call-update) | async-done | bytes 1048592 | tf_op jit(solution)/shard_map/psum | solution.py:85
  92.9 2.0 fusion.14
  94.9 1.0 copy-done.2
  95.9 1.4 fusion.16
  97.3 16.4 %gather_fusion = bf16[1024,4096]{1,0:T(8,128)(2,1)} fusion(bf16[128,4096]{1,0:T(8,128)(2,1)} %fusion.16, s32[1024]{0:T(1024)S(1)} %broadcast_clamp_fusion.1), kind=kCustom, calls=%fused_computation | custom fusion | bytes 16781312 | tf_op jit(solution)/shard_map/gather | solution.py:104
  113.7 22.1 %scatter_custom_fusion = bf16[2048,4096]{1,0:T(8,128)(2,1)} fusion(s32[1024]{0:T(1024)S(1)} %bitcast.150, bf16[1024,4096]{1,0:T(8,128)(2,1)} %gather_fusion, bf16[]{:T(256)} %constant.49.clone.1), kind=kCustom, calls=%fused_computation.15 | custom fusion | bytes 16777728 | tf_op jit(solution)/shard_map/scatter | solution.py:104
  135.8 191.9 %all_to_all.10 = bf16[64,32,4096]{2,1,0:T(8,128)(2,1)} all-to-all(bf16[64,32,4096]{2,1,0:T(8,128)(2,1)} %bitcast.140), channel_id=1, replica_groups=mesh['ep'=32,'tp'=4] {'ep'}, dimensions={0} | all-to-all | bytes 33554432 | tf_op jit(solution)/shard_map/all_to_all | solution.py:107
  327.8 12.5 %fusion.3 = f32[2,32,32,192]{3,2,1,0:T(8,128)} fusion(bf16[32,2,32,4096]{3,2,1,0:T(8,128)(2,1)} %bitcast.141, bf16[2,4096,192]{1,2,0:T(8,128)(2,1)} %param.27), kind=kOutput, calls=%fused_computation.10 | convolution fusion | flops 3221225472 | bytes 21495808 | tf_op jit(solution)/shard_map/secd,edf->secf/dot_general | solution.py:112
  340.3 10.5 %fusion.17 = bf16[32,2,32,192]{3,2,0,1:T(8,128)(2,1)} fusion(f32[2,32,32,192]{3,2,1,0:T(8,128)} %fusion.3, bf16[2,4096,192]{1,2,0:T(8,128)(2,1)} %param.28, bf16[32,2,32,4096]{3,2,1,0:T(8,128)(2,1)} %bitcast.142), kind=kOutput, calls=%fused_computation.29 | convolution fusion | flops 3223584768 | bytes 22282240 | tf_op jit(solution)/shard_map/secd,edf->secf/dot_general | solution.py:113
  350.8 9.3 %convert_bitcast_fusion = bf16[32,2,32,4096]{3,2,0,1:T(8,128)(2,1)} fusion(bf16[32,2,32,192]{3,2,0,1:T(8,128)(2,1)} %fusion.17, bf16[2,192,4096]{2,1,0:T(8,128)(2,1)S(1)} %copy-done), kind=kOutput, calls=%fused_computation.4 | convolution fusion | flops 3229614080 | bytes 20709376 | tf_op jit(solution)/shard_map/secf,efd->secd/dot_general | solution.py:115
  360.1 0.0 reduce-scatter.2.cloned.1.call-update
  360.1 146.7 %reduce-scatter.2.cloned.1.call-done = bf16[32,2,32,1024]{3,2,0,1:T(8,128)(2,1)} async-done(((bf16[32,2,32,4096]{3,2,0,1:T(8,128)(2,1)}), bf16[32,2,32,1024]{3,2,0,1:T(8,128)(2,1)}) %reduce-scatter.2.cloned.1.call-update) | async-done | bytes 4194320 | tf_op jit(solution)/shard_map/reduce_scatter | solution.py:116
  506.8 5.0 copy.50
  511.8 8.0 %all-to-all-start.1 = ((bf16[64,32,1024]{2,1,0:T(8,128)(2,1)}), bf16[64,32,1024]{2,1,0:T(8,128)(2,1)}, u32[]{:S(2)}, u32[]{:S(2)}) async-start(bf16[64,32,1024]{2,1,0:T(8,128)(2,1)} %bitcast.143), calls=%async_computation.2 | async-start | bytes 8388608 | tf_op jit(solution)/shard_map/all_to_all | solution.py:118
  519.8 0.1 copy.51
  519.9 53.9 %all-to-all-done.1 = bf16[64,32,1024]{2,1,0:T(8,128)(2,1)} async-done(((bf16[64,32,1024]{2,1,0:T(8,128)(2,1)}), bf16[64,32,1024]{2,1,0:T(8,128)(2,1)}, u32[]{:S(2)}, u32[]{:S(2)}) %all-to-all-start.1) | async-done | bytes 4194336 | tf_op jit(solution)/shard_map/all_to_all | solution.py:118
  573.8 8.8 %gather_fusion.1 = bf16[1024,1024]{1,0:T(8,128)(2,1)} fusion(bf16[2048,1024]{1,0:T(8,128)(2,1)} %bitcast.37, s32[1024]{0:T(1024)S(1)} %broadcast_clamp_fusion), kind=kCustom, calls=%fused_computation.1 | custom fusion | bytes 4198400 | tf_op jit(solution)/shard_map/gather | solution.py:119
  582.6 2.9 fusion.10
  585.5 1.7 add_convert_fusion.1
  (31 shorter events, 0.1 us)
Async XLA Ops:
  6.5 344.3 %copy-start = (bf16[2,192,4096]{2,1,0:T(8,128)(2,1)S(1)}, bf16[2,192,4096]{2,1,0:T(8,128)(2,1)}, u32[]{:S(2)}) copy-start(bf16[2,192,4096]{2,1,0:T(8,128)(2,1)} %param.29) | copy-start | bytes 9437188
  6.5 86.3 %all-reduce.2.cloned.1.call-start = ((), (), s32[]{:S(2)}) async-start(), calls=%async_computation.3 | async-start | bytes 2097152 | tf_op jit(solution)/shard_map/psum | solution.py:85
  9.2 9.7 %copy-start.1 = (pred[128,4096]{0,1:T(8,128)(4,1)}, pred[128,4096]{0,1:T(8,128)(4,1)S(1)}, u32[]{:S(2)}) copy-start(pred[128,4096]{0,1:T(8,128)(4,1)S(1)} %bitcast_and_fusion) | copy-start | bytes 1572868
  9.2 9.7 %copy-start.4 = (bf16[128,1024]{1,0:T(8,128)(2,1)S(1)}, bf16[128,1024]{1,0:T(8,128)(2,1)}, u32[]{:S(2)}) copy-start(bf16[128,1024]{1,0:T(8,128)(2,1)} %param.16) | copy-start | bytes 786436
  9.2 9.7 %copy-start.5 = (bf16[128,128]{1,0:T(8,128)(2,1)S(1)}, bf16[128,128]{1,0:T(8,128)(2,1)}, u32[]{:S(2)}) copy-start(bf16[128,128]{1,0:T(8,128)(2,1)} %param.17) | copy-start | bytes 98308
  30.3 8.5 %copy-start.3 = (f32[128,1,8,128]{0,3,2,1:T(8,128)S(1)}, f32[128,1,8,128]{0,3,2,1:T(8,128)}, u32[]{:S(2)}) copy-start(f32[128,1,8,128]{0,3,2,1:T(8,128)} %get-tuple-element.10) | copy-start | bytes 1572868
  30.3 8.5 %copy-start.9 = (bf16[128,128]{1,0:T(8,128)(2,1)S(1)}, bf16[128,128]{1,0:T(8,128)(2,1)}, u32[]{:S(2)}) copy-start(bf16[128,128]{1,0:T(8,128)(2,1)} %param.18) | copy-start | bytes 98308
  38.8 6.6 %copy-start.6 = (s32[128,8]{0,1:T(8,128)S(1)}, s32[128,8]{0,1:T(8,128)}, u32[]{:S(2)}) copy-start(s32[128,8]{0,1:T(8,128)} %param.25) | copy-start | bytes 12292
  38.8 6.9 %copy-start.7 = (bf16[4096]{0:T(1024)(128)(2,1)S(1)}, bf16[4096]{0:T(1024)(128)(2,1)}, u32[]{:S(2)}) copy-start(bf16[4096]{0:T(1024)(128)(2,1)} %param.24) | copy-start | bytes 24580
  44.9 461.9 %reduce-scatter.2.cloned.1.call-start = ((), (), s32[]{:S(2)}) async-start(), calls=%async_computation.4 | async-start | bytes 20971520 | tf_op jit(solution)/shard_map/reduce_scatter | solution.py:116
  94.9 1.0 copy-start.2
  360.1 159.6 %copy-start.8 = (f32[128,8]{0,1:T(8,128)S(1)}, f32[128,8]{0,1:T(8,128)}, u32[]{:S(2)}) copy-start(f32[128,8]{0,1:T(8,128)} %param.26) | copy-start | bytes 12292
  511.8 62.1 %all-to-all-start.1 = ((bf16[64,32,1024]{2,1,0:T(8,128)(2,1)}), bf16[64,32,1024]{2,1,0:T(8,128)(2,1)}, u32[]{:S(2)}, u32[]{:S(2)}) async-start(bf16[64,32,1024]{2,1,0:T(8,128)(2,1)} %bitcast.143), calls=%async_computation.2 | async-start | bytes 8388608 | tf_op jit(solution)/shard_map/all_to_all | solution.py:118
Sparse Core Ops, SparseCore 0:
  45.0 47.8 all-reduce.1
  360.2 146.5 reduce-scatter.1
where the time goes:
time: 604 us; the launch traced here: 594 us
  waiting for transfers between devices  213 us (35%)
  blocking collectives  192 us (32%)
  matrix products  57.5 us (10%)
  local copies, waits for them, and re-layouts  56.7 us (9%)
  other arithmetic  52.4 us (9%)
  between operations  13.9 us (2%)
  starting transfers between devices  8.57 us (1%)
    all_to_all x1, blocking collectives, on_device(): lax.all_to_all(outgoing, 'ep', split_axis=0, concat_axis=0, tiled=True)  192 us
    reduce_scatter x1, waiting for transfers between devices, on_device(): lax.psum_scatter(down_part.astype(jnp.bfloat16), 'tp', scatter_dimension=...  147 us
    all_to_all x1, waiting for transfers between devices, on_device(): lax.all_to_all(summed, 'ep', split_axis=0, concat_axis=0, tiled=True)  53.9 us
    another operation x4, other arithmetic  32.2 us
    scatter x1, local copies, waits for them, and re-layouts, on_device(): outgoing = jnp.zeros((experts * capacity, normed.shape[1]), jnp.bfloat16)...  22.1 us
    gather x1, local copies, waits for them, and re-layouts, on_device(): normed[token_of]  16.4 us
    psum x1, waiting for transfers between devices, on_device(): lax.psum(partial_proj.astype(jnp.bfloat16), 'tp').astype(jnp.float32)  12.8 us
    dot_general x1, matrix products, on_device(): jnp.einsum('secd,edf->secf', rows_in, w_gate, preferred_element_type=jnp....  12.5 us
  transfers between devices with their start and end apart: 3, of which 3 were waited for; matrix products, arithmetic and copies ran while one was open for 6% of the time, Pallas kernels for 0%

commit v1 on v0

v1 whole, which is shorter than its diff:
```python
import functools

import jax
import jax.numpy as jnp
from jax import lax
from jax.experimental import pallas as pl
from jax.experimental.pallas import tpu as pltpu
from jax.sharding import PartitionSpec as P

D = 4096
HD = 128
TOK = 128
CAP = 32
META = 16

norm_eps = 1e-06
neg_fill = -1e30
f32 = jnp.float32
bf16 = jnp.bfloat16
VMEM_LIMIT = 56 * 1024 * 1024


def dot(a, b, contract=((1,), (0,)), precision=None):
    return lax.dot_general(
        a, b, (contract, ((), ())), preferred_element_type=f32, precision=precision
    )


def params(*semantics):
    return pltpu.CompilerParams(
        vmem_limit_bytes=VMEM_LIMIT, dimension_semantics=semantics or None
    )


def attend_kernel(
    count_ref, len_ref, q_ref, nk_ref, nv_ref, ck_ref, cv_ref, proj_hbm, down_hbm,
    out_ref, down_out, attended, proj, sem, down_sem,
):
    parts = out_ref.shape[0]
    width = out_ref.shape[2]
    heads = q_ref.shape[1] // HD
    convs, depth = ck_ref.shape[0], ck_ref.shape[1]
    fetch = pltpu.make_async_copy(proj_hbm, proj, sem)
    fetch.start()
    regroup = [
        pltpu.make_async_copy(
            down_hbm.at[:, :, pl.ds(j * width, width)], down_out.at[j], down_sem.at[j]
        )
        for j in range(parts)
    ]
    for copy in regroup:
        copy.start()
    ends = []
    total = jnp.int32(0)
    for c in range(convs):
        total = total + count_ref[c]
        ends.append(total)
    to_exp2 = HD ** (-0.5) * 1.4426950408889634
    block = 32
    rows = heads * block
    row_tok = lax.broadcasted_iota(jnp.int32, (rows, 1), 0) % block
    col_tok = lax.broadcasted_iota(jnp.int32, (1, TOK), 1)

    def conv_of(position):
        return sum((position >= end).astype(jnp.int32) for end in ends)

    col_conv = conv_of(col_tok)
    key_pos = lax.broadcasted_iota(jnp.int32, (rows, depth), 1)
    for b in range(TOK // block):
        start = b * block
        q = jnp.concatenate(
            [q_ref[start : start + block, h * HD : (h + 1) * HD] for h in range(heads)], axis=0
        )
        tok = row_tok + start
        row_conv = conv_of(tok)
        s = dot(q, nk_ref[...], ((1,), (1,)))
        s = jnp.where((row_conv == col_conv) & (col_tok <= tok), s, neg_fill)
        top = jnp.max(s, axis=1, keepdims=True)
        p = jnp.exp2((s - top) * to_exp2)
        denom = jnp.sum(p, axis=1, keepdims=True)
        acc = dot(p.astype(bf16), nv_ref[...])
        first = conv_of(jnp.int32(start))
        last = conv_of(jnp.int32(start + block - 1))

        def step(c, carry, q=q, row_conv=row_conv):
            top, denom, acc = carry
            s = dot(q, ck_ref[c], ((1,), (1,)))
            limit = jnp.where(row_conv == c, len_ref[c], 0)
            s = jnp.where(key_pos < limit, s, neg_fill)
            new_top = jnp.maximum(top, jnp.max(s, axis=1, keepdims=True))
            p = jnp.exp2((s - new_top) * to_exp2)
            alpha = jnp.exp2((top - new_top) * to_exp2)
            denom = denom * alpha + jnp.sum(p, axis=1, keepdims=True)
            acc = acc * alpha + dot(p.astype(bf16), cv_ref[c])
            return new_top, denom, acc

        top, denom, acc = lax.fori_loop(first, last + 1, step, (top, denom, acc))
        out = (acc / denom).astype(bf16)
        for h in range(heads):
            attended[start : start + block, h * HD : (h + 1) * HD] = out[
                h * block : (h + 1) * block
            ]
    fetch.wait()
    for j in range(parts):
        out_ref[j] = dot(attended[...], proj[:, j * width : (j + 1) * width]).astype(bf16)
    for copy in regroup:
        copy.wait()


def attend(queries, new_keys, new_values, cache_keys, cache_values, new_count, cached_len, out_proj, w_down, parts):
    width = D // parts
    vmem = pl.BlockSpec(memory_space=pltpu.VMEM)
    smem = pl.BlockSpec(memory_space=pltpu.SMEM)
    hbm = pl.BlockSpec(memory_space=pl.ANY)
    return pl.pallas_call(
        attend_kernel,
        out_shape=(
            jax.ShapeDtypeStruct((parts, TOK, width), bf16),
            jax.ShapeDtypeStruct((parts,) + w_down.shape[:2] + (width,), bf16),
        ),
        in_specs=[smem, smem, vmem, vmem, vmem, vmem, vmem, hbm, hbm],
        out_specs=(vmem, hbm),
        scratch_shapes=[
            pltpu.VMEM((TOK, queries.shape[1]), bf16),
            pltpu.VMEM(out_proj.shape, bf16),
            pltpu.SemaphoreType.DMA,
            pltpu.SemaphoreType.DMA((parts,)),
        ],
        compiler_params=params(),
        name="attend",
    )(new_count, cached_len, queries, new_keys, new_values, cache_keys, cache_values, out_proj, w_down)


def thirds(v):
    high = v.astype(bf16).astype(f32)
    mid = (v - high).astype(bf16).astype(f32)
    return high, mid, v - high - mid


def prepare_kernel(at_ref, terms_ref, residual_ref, gain_ref, ids_ref, gate_ref, payload_ref, stream_ref):
    del at_ref
    total = residual_ref[...].astype(f32)
    terms = sum(terms_ref[j].astype(f32) for j in range(terms_ref.shape[0]))
    stream = (total + terms).astype(bf16)
    stream_ref[...] = stream
    s = stream.astype(f32)
    payload_ref[:TOK] = (s * gain_ref[...].astype(f32)).astype(bf16)
    square = jnp.sum(s * s, axis=1, keepdims=True)
    diagonal = lax.broadcasted_iota(jnp.int32, (TOK, TOK), 0) == lax.broadcasted_iota(
        jnp.int32, (TOK, TOK), 1
    )
    square = jnp.sum(jnp.where(diagonal, square, 0.0), axis=0, keepdims=True)
    topk = ids_ref.shape[0]

    def in_line(v):
        return jnp.concatenate([v[k : k + 1] for k in range(topk)], axis=1)

    gate = thirds(in_line(gate_ref[...]))
    blank = jnp.zeros((1, (topk - 3) * TOK), f32)
    squares = jnp.concatenate(list(thirds(square)) + [blank], axis=1)
    lines = [in_line(ids_ref[...].astype(f32)), *gate, squares]
    lines.append(jnp.zeros((META - len(lines), topk * TOK), f32))
    payload_ref[TOK:] = jnp.concatenate(lines, axis=0).astype(bf16)


def prepare(at, terms, residual, gain, ids_t, gate_t):
    width = terms.shape[2]
    return pl.pallas_call(
        prepare_kernel,
        out_shape=(
            jax.ShapeDtypeStruct((TOK + META, width), bf16),
            jax.ShapeDtypeStruct((TOK, width), bf16),
        ),
        grid_spec=pltpu.PrefetchScalarGridSpec(
            num_scalar_prefetch=1,
            grid=(1,),
            in_specs=[
                pl.BlockSpec(terms.shape, lambda i, at: (0, 0, 0)),
                pl.BlockSpec((TOK, width), lambda i, at: (0, at[0])),
                pl.BlockSpec((1, width), lambda i, at: (0, at[0])),
                pl.BlockSpec(ids_t.shape, lambda i, at: (0, 0)),
                pl.BlockSpec(gate_t.shape, lambda i, at: (0, 0)),
            ],
            out_specs=[
                pl.BlockSpec((TOK + META, width), lambda i, at: (0, 0)),
                pl.BlockSpec((TOK, width), lambda i, at: (0, 0)),
            ],
        ),
        compiler_params=params("arbitrary"),
        name="prepare",
    )(at, terms, residual, gain, ids_t, gate_t)


def experts_kernel(first_ref, x_ref, gate_w_ref, up_w_ref, act_ref, rows, groups, parts):
    width = x_ref.shape[2]
    topk = width // TOK
    local = gate_w_ref.shape[0]
    hidden = gate_w_ref.shape[2]
    earlier = (
        lax.broadcasted_iota(jnp.int32, (TOK, TOK), 0)
        < lax.broadcasted_iota(jnp.int32, (TOK, TOK), 1)
    ).astype(bf16)
    slots = lax.broadcasted_iota(jnp.int32, (CAP, TOK), 0).astype(f32)
    scales = [[], []]
    gates = [[], []]
    for g in range(groups):
        meta = x_ref[g * parts, TOK:].astype(f32)
        square = jnp.zeros((1, TOK), f32)
        for q in range(parts):
            line = (meta if q == 0 else x_ref[g * parts + q, TOK:].astype(f32))[4:5]
            square = square + (line[:, :TOK] + line[:, TOK : 2 * TOK] + line[:, 2 * TOK : 3 * TOK])
        scale = lax.rsqrt(square / D + norm_eps)
        ids = meta[0:1]
        gate = meta[1:2] + meta[2:3] + meta[3:4]
        members, weights = [], []
        for e in range(local):
            hit = ids == (first_ref[0] + e).astype(f32)
            ones = jnp.where(hit, 1.0, 0.0)
            weight = jnp.where(hit, gate, 0.0)
            members.append(sum(ones[:, k * TOK : (k + 1) * TOK] for k in range(topk)))
            weights.append(sum(weight[:, k * TOK : (k + 1) * TOK] for k in range(topk)))
        named = jnp.concatenate(members + [jnp.zeros((8 - local, TOK), f32)], axis=0)
        slot = dot(named.astype(bf16), earlier)
        picks = []
        for e in range(local):
            pick = (slots == slot[e : e + 1]) & (members[e] > 0.5)
            picks.append(jnp.where(pick, 1.0, 0.0))
            scales[e].append(jnp.sum(jnp.where(pick, scale, 0.0), axis=1, keepdims=True))
            gates[e].append(jnp.sum(jnp.where(pick, weights[e], 0.0), axis=1, keepdims=True))
        picks = jnp.concatenate(picks, axis=0).astype(bf16)
        for q in range(parts):
            picked = dot(picks, x_ref[g * parts + q, :TOK]).astype(bf16)
            for e in range(local):
                rows[e, g * CAP : (g + 1) * CAP, q * width : (q + 1) * width] = picked[
                    e * CAP : (e + 1) * CAP
                ]
    done = []
    for e in range(local):
        scale = jnp.concatenate(scales[e], axis=0)
        gate_part = dot(rows[e], gate_w_ref[e]) * scale
        up_part = dot(rows[e], up_w_ref[e]) * scale
        silu = gate_part / (1.0 + jnp.exp(-gate_part))
        done.append((silu * up_part * jnp.concatenate(gates[e], axis=0)).astype(bf16))
    act_ref[...] = jnp.concatenate(done, axis=1)


def run_experts(first, gathered, w_gate, w_up, parts):
    groups = 4
    total = gathered.shape[0] // parts
    local, _, hidden = w_gate.shape
    whole = pl.BlockSpec(w_gate.shape, lambda i: (0, 0, 0), pipeline_mode=pl.Buffered(1))
    return pl.pallas_call(
        functools.partial(experts_kernel, groups=groups, parts=parts),
        out_shape=jax.ShapeDtypeStruct((total * CAP, local * hidden), bf16),
        grid=(total // groups,),
        in_specs=[
            pl.BlockSpec(memory_space=pltpu.SMEM),
            pl.BlockSpec((groups * parts,) + gathered.shape[1:], lambda i: (i, 0, 0)),
            whole,
            whole,
        ],
        out_specs=pl.BlockSpec((groups * CAP, local * hidden), lambda i: (i, 0)),
        scratch_shapes=[pltpu.VMEM((local, groups * CAP, D), bf16)],
        compiler_params=params("arbitrary"),
        name="experts",
    )(first, gathered, w_gate, w_up)


def down_kernel(act_ref, w_ref, out_ref):
    parts, local, hidden, width = w_ref.shape
    groups = out_ref.shape[0]
    for e in range(local):
        total = sum(
            dot(act_ref[q, :, e * hidden : (e + 1) * hidden], w_ref[q, e]) for q in range(parts)
        )
        out_ref[:, e * CAP : (e + 1) * CAP] = total.astype(bf16).reshape(groups, CAP, width)


def run_down(act, w):
    parts, local, hidden, width = w.shape
    groups = 8
    total = act.shape[1] // CAP
    return pl.pallas_call(
        down_kernel,
        out_shape=jax.ShapeDtypeStruct((total, local * CAP, width), bf16),
        grid=(total // groups,),
        in_specs=[
            pl.BlockSpec((parts, groups * CAP, act.shape[2]), lambda i: (0, i, 0)),
            pl.BlockSpec(w.shape, lambda i: (0, 0, 0, 0), pipeline_mode=pl.Buffered(1)),
        ],
        out_specs=pl.BlockSpec((groups, local * CAP, width), lambda i: (i, 0, 0)),
        compiler_params=params("arbitrary"),
        name="down",
    )(act, w)


def combine_kernel(ids_ref, rows_ref, stream_ref, out_ref):
    slots = rows_ref.shape[0]
    experts = slots // CAP
    ids = ids_ref[...]
    names = lax.broadcasted_iota(jnp.int32, (TOK, experts), 1)
    member = sum((ids[:, k : k + 1] == names).astype(f32) for k in range(ids.shape[1]))
    earlier = (
        lax.broadcasted_iota(jnp.int32, (TOK, TOK), 1)
        < lax.broadcasted_iota(jnp.int32, (TOK, TOK), 0)
    ).astype(bf16)
    place = (dot(earlier, member.astype(bf16)) + 1.0) * member
    spread = (
        lax.broadcasted_iota(jnp.int32, (experts, slots), 1) // CAP
        == lax.broadcasted_iota(jnp.int32, (experts, slots), 0)
    ).astype(bf16)
    place = dot(place.astype(bf16), spread)
    own = (lax.broadcasted_iota(jnp.int32, (TOK, slots), 1) % CAP + 1).astype(f32)
    picks = (place == own).astype(bf16)
    out_ref[...] = (stream_ref[...].astype(f32) + dot(picks, rows_ref[...])).astype(bf16)


def combine(ids, rows, stream):
    vmem = pl.BlockSpec(memory_space=pltpu.VMEM)
    return pl.pallas_call(
        combine_kernel,
        out_shape=jax.ShapeDtypeStruct(stream.shape, bf16),
        in_specs=[vmem] * 3,
        out_specs=vmem,
        compiler_params=params(),
        name="combine",
    )(ids, rows, stream)


def on_device(
    residual,
    queries,
    new_keys,
    new_values,
    cache_keys,
    cache_values,
    new_count,
    cached_len,
    out_proj,
    norm_gain,
    expert_ids,
    gate_scale,
    w_gate,
    w_up,
    w_down,
):
    parts = lax.axis_size("tp")
    at = lax.axis_index("tp").astype(jnp.int32).reshape(1)
    first = (lax.axis_index("ep") * w_gate.shape[0]).astype(jnp.int32).reshape(1)
    terms, down_parts = attend(
        queries, new_keys, new_values, cache_keys, cache_values, new_count, cached_len,
        out_proj, w_down, parts,
    )
    terms = lax.all_to_all(terms, "tp", split_axis=0, concat_axis=0, tiled=True)
    down_w = lax.all_to_all(down_parts, "tp", split_axis=0, concat_axis=0, tiled=True)
    payload, stream = prepare(
        at, terms, residual, norm_gain.reshape(1, D), expert_ids.T, gate_scale.T
    )
    gathered = lax.all_gather(payload, ("ep", "tp"))
    act = run_experts(first, gathered, w_gate, w_up, parts)
    act = lax.all_gather(act, "tp")
    rows = run_down(act, down_w)
    rows = lax.all_to_all(rows, "ep", split_axis=0, concat_axis=0, tiled=True)
    return combine(expert_ids, rows.reshape(-1, rows.shape[2]), stream)


def solution(mesh):
    in_specs = (
        P("ep", None),
        P("ep", "tp"),
        P("ep", "tp"),
        P("ep", "tp"),
        P("ep", None, "tp"),
        P("ep", None, "tp"),
        P("ep"),
        P("ep"),
        P("tp", None),
        P(),
        P("ep", None),
        P("ep", None),
        P("ep", None, "tp"),
        P("ep", None, "tp"),
        P("ep", "tp", None),
    )
    out_specs = P("ep", "tp")
    return jax.shard_map(
        on_device, mesh=mesh, in_specs=in_specs, out_specs=out_specs, check_vma=False
    )
```

time: 604 us -> 416 us (0.69); the launches traced: 594 us -> 415 us
  Pallas kernels: 0 us -> 140 us
  blocking collectives: 192 us -> 67 us
  matrix products: 57.5 us -> 0 us
  other arithmetic: 52.4 us -> 0 us
  local copies, waits for them, and re-layouts: 56.7 us -> 12.6 us
  waiting for transfers between devices: 213 us -> 171 us
    reduce_scatter x1 -> x0, waiting for transfers between devices: 147 us -> none  [on_device(): lax.psum_scatter(down_part.astype(jnp.bfloat16), 'tp', scatter_dimension=...]
    pallas_call x0 -> x5, Pallas kernels: none -> 140 us  [the longest x1 99.1 us: attend(): pl.pallas_call(attend_kernel, out_shape=(jax.ShapeDtypeStruct((parts, TOK...]
    all_to_all x1, blocking collectives: 192 us -> 67 us  [on_device(): lax.all_to_all(down_parts, 'tp', split_axis=0, concat_axis=0, tiled=True)]
    all_gather x0 -> x2, waiting for transfers between devices: none -> 102 us  [the longest x1 102 us: on_device(): gathered = lax.all_gather(payload, ('ep', 'tp'))]
    dot_general x8 -> x0, matrix products: 57.5 us -> none  [the longest x1 12.5 us: on_device(): jnp.einsum('secd,edf->secf', rows_in, w_gate, preferred_element_type=jnp....]
    another operation x4 -> x0, other arithmetic: 32.2 us -> none
    gather x2 -> x0, local copies, waits for them, and re-layouts: 25.2 us -> none  [the longest x1 16.4 us: on_device(): normed[token_of]]
    scatter x1 -> x0, local copies, waits for them, and re-layouts: 22.1 us -> none  [on_device(): outgoing = jnp.zeros((experts * capacity, normed.shape[1]), jnp.bfloat16)...]
  transfers between devices with their start and end apart: 3 -> 4, of which waited for: 3 -> 3; matrix products, arithmetic and copies ran while one was open for 6% -> 3% of each run, Pallas kernels for 0% -> 0%
where the time goes in v1:
time: 416 us; the launch traced here: 415 us
  waiting for transfers between devices  171 us (41%)
  Pallas kernels  140 us (34%)
  blocking collectives  67 us (16%)
  between operations  13.4 us (3%)
  local copies, waits for them, and re-layouts  12.6 us (3%)
  starting transfers between devices  12 us (3%)
    all_gather x1, waiting for transfers between devices, on_device(): gathered = lax.all_gather(payload, ('ep', 'tp'))  102 us
    pallas_call x1, Pallas kernels, attend(): pl.pallas_call(attend_kernel, out_shape=(jax.ShapeDtypeStruct((parts, TOK...  99.1 us
    all_to_all x1, blocking collectives, on_device(): lax.all_to_all(down_parts, 'tp', split_axis=0, concat_axis=0, tiled=True)  67 us
    all_to_all x1, waiting for transfers between devices, on_device(): rows = lax.all_to_all(rows, 'ep', split_axis=0, concat_axis=0, tiled=True)  53.8 us
    pallas_call x1, Pallas kernels, run_experts(): pl.pallas_call(functools.partial(experts_kernel, groups=groups, parts=par...  25.9 us
    all_to_all x1, waiting for transfers between devices, on_device(): terms = lax.all_to_all(terms, 'tp', split_axis=0, concat_axis=0, tiled=True)  14.5 us
    unnamed x13, local copies, waits for them, and re-layouts  11.9 us
    pallas_call x1, Pallas kernels, run_down(): pl.pallas_call(down_kernel, out_shape=jax.ShapeDtypeStruct((total, local...  8.48 us
  transfers between devices with their start and end apart: 4, of which 3 were waited for; matrix products, arithmetic and copies ran while one was open for 3% of the time, Pallas kernels for 0%

profile of v1, /device:TPU:32, one launch (start us, length us, event | category | flops | bytes accessed | tf_op | source)
XLA Modules:
  0.0 415.5 jit_solution(18145869548901990854)
XLA Ops:
  6.5 0.0 copy-start.4
  6.5 99.1 %attend.1 = (bf16[4,128,1024]{2,1,0:T(8,128)(2,1)}, bf16[4,2,192,1024]{3,2,1,0:T(8,128)(2,1)}) custom-call(s32[4]{0:T(128)} %count_ref.1, s32[4]{0:T(128)} %len_ref.1, bf16[128,1024]{1,0:T(8,128)(2,1)} %q_ref.1, bf16[128,128]{1,0:T(8,128)(2,1)} %nk_ref.1, bf16[128,128]{1,0:T(8,128)(2,1)} %nv_ref.1, bf16[4,1024,128]{2,1,0:T(8,128)(2,1)} %ck_ref.1, ...), custom_call_target="tpu_custom_call" | custom-call | tf_op jit(solution)/shard_map/attend/pallas_call | solution.py:115
  105.6 4.3 %all-to-all-start = ((bf16[4,128,1024]{2,1,0:T(8,128)(2,1)}), bf16[4,128,1024]{2,1,0:T(8,128)(2,1)S(1)}, u32[]{:S(2)}, u32[]{:S(2)}) async-start(bf16[4,128,1024]{2,1,0:T(8,128)(2,1)} %get-tuple-element.9), calls=%async_computation | async-start | bytes 2097152 | tf_op jit(solution)/shard_map/all_to_all | solution.py:354
  109.9 0.0 all-gather.5.cloned.1.call-start
  109.9 0.0 copy-done.4
  109.9 0.6 reshape.14.gain_ref
  110.6 14.5 %all-to-all-done.terms_ref = bf16[4,128,1024]{2,1,0:T(8,128)(2,1)S(1)} async-done(((bf16[4,128,1024]{2,1,0:T(8,128)(2,1)}), bf16[4,128,1024]{2,1,0:T(8,128)(2,1)S(1)}, u32[]{:S(2)}, u32[]{:S(2)}) %all-to-all-start) | async-done | bytes 1048608 | tf_op jit(solution)/shard_map/all_to_all | solution.py:354
  125.0 0.0 copy-start
  125.0 1.0 copy-done
  126.0 2.4 prepare.1
  128.4 0.0 copy-start.1
  128.4 0.0 all-gather.5.cloned.1.call-update
  128.4 0.0 all-gather.7.cloned.1.call-start
  128.5 6.2 %copy.16.gate_w_ref = bf16[2,4096,192]{2,1,0:T(8,128)(2,1)} copy(bf16[2,4096,192]{1,2,0:T(8,128)(2,1)} %param.27) | data formatting | bytes 6291456 | tf_op args[12]
  134.7 0.0 copy-done.1
  134.7 4.0 copy.17.up_w_ref
  138.7 102.2 %all-gather.5.cloned.1.call-done = bf16[18432,1024]{1,0:T(8,128)(2,1)} async-done(((bf16[144,1024]{1,0:T(8,128)(2,1)}), bf16[18432,1024]{1,0:T(8,128)(2,1)}) %all-gather.5.cloned.1.call-update) | async-done | bytes 37748752 | tf_op jit(solution)/shard_map/all_gather | solution.py:359
  240.9 0.0 copy-start.2
  240.9 25.9 %experts.1 = bf16[1024,384]{1,0:T(8,128)(2,1)} custom-call(s32[1]{0:T(128)} %bitcast.first_ref, bf16[128,144,1024]{2,1,0:T(8,128)(2,1)} %bitcast.7, bf16[2,4096,192]{2,1,0:T(8,128)(2,1)} %copy.16.gate_w_ref, bf16[2,4096,192]{2,1,0:T(8,128)(2,1)} %copy.17.up_w_ref), custom_call_target="tpu_custom_call" | custom-call | tf_op jit(solution)/shard_map/experts/pallas_call | solution.py:252
  266.8 0.0 all-gather.7.cloned.1.call-update
  266.8 0.0 copy-done.2
  266.9 67.0 %all_to_all.15.w_ref = bf16[4,2,192,1024]{3,2,1,0:T(8,128)(2,1)} all-to-all(bf16[4,2,192,1024]{3,2,1,0:T(8,128)(2,1)S(1)} %copy-done.2), channel_id=1, replica_groups=mesh['ep'=32,'tp'=4] {'tp'}, dimensions={0} | all-to-all | bytes 6291456 | tf_op jit(solution)/shard_map/all_to_all | solution.py:355
  333.8 0.0 all-gather.7.cloned.1.call-done
  333.8 8.5 %down.1 = bf16[32,64,1024]{2,1,0:T(8,128)(2,1)} custom-call(bf16[4,1024,384]{2,1,0:T(8,128)(2,1)} %bitcast.8, bf16[4,2,192,1024]{3,2,1,0:T(8,128)(2,1)} %all_to_all.15.w_ref), custom_call_target="tpu_custom_call" | custom-call | tf_op jit(solution)/shard_map/down/pallas_call | solution.py:283
  342.3 0.0 copy-start.3
  342.3 7.6 %all-to-all-start.2 = ((bf16[32,64,1024]{2,1,0:T(8,128)(2,1)}), bf16[32,64,1024]{2,1,0:T(8,128)(2,1)}, u32[]{:S(2)}, u32[]{:S(2)}) async-start(bf16[32,64,1024]{2,1,0:T(8,128)(2,1)} %down.1), calls=%async_computation.2 | async-start | bytes 8388608 | tf_op jit(solution)/shard_map/all_to_all | solution.py:363
  349.9 0.0 copy-done.3
  349.9 0.7 copy.18.ids_ref
  350.7 53.8 %all-to-all-done.2 = bf16[32,64,1024]{2,1,0:T(8,128)(2,1)} async-done(((bf16[32,64,1024]{2,1,0:T(8,128)(2,1)}), bf16[32,64,1024]{2,1,0:T(8,128)(2,1)}, u32[]{:S(2)}, u32[]{:S(2)}) %all-to-all-start.2) | async-done | bytes 4194336 | tf_op jit(solution)/shard_map/all_to_all | solution.py:363
  404.5 4.2 %combine.1 = bf16[128,1024]{1,0:T(8,128)(2,1)} custom-call(s32[128,8]{1,0:T(8,128)} %copy.18.ids_ref, bf16[2048,1024]{1,0:T(8,128)(2,1)} %bitcast.6.rows_ref, bf16[128,1024]{1,0:T(8,128)(2,1)} %get-tuple-element.12.stream_ref), custom_call_target="tpu_custom_call" | custom-call | tf_op jit(solution)/shard_map/combine/pallas_call | solution.py:320
Async XLA Ops:
  6.5 103.4 %copy-start.4 = (bf16[4096]{0:T(1024)(128)(2,1)S(1)}, bf16[4096]{0:T(1024)(128)(2,1)}, u32[]{:S(2)}) copy-start(bf16[4096]{0:T(1024)(128)(2,1)} %param.24) | copy-start | bytes 24580
  105.6 19.4 %all-to-all-start = ((bf16[4,128,1024]{2,1,0:T(8,128)(2,1)}), bf16[4,128,1024]{2,1,0:T(8,128)(2,1)S(1)}, u32[]{:S(2)}, u32[]{:S(2)}) async-start(bf16[4,128,1024]{2,1,0:T(8,128)(2,1)} %get-tuple-element.9), calls=%async_computation | async-start | bytes 2097152 | tf_op jit(solution)/shard_map/all_to_all | solution.py:354
  109.9 131.0 %all-gather.5.cloned.1.call-start = ((), (), s32[]{:S(2)}) async-start(), calls=%async_computation.3 | async-start | bytes 38043648 | tf_op jit(solution)/shard_map/all_gather | solution.py:359
  125.0 1.0 copy-start
  128.4 6.3 %copy-start.1 = (bf16[2,4096,192]{1,2,0:T(8,128)(2,1)S(1)}, bf16[2,4096,192]{1,2,0:T(8,128)(2,1)}, u32[]{:S(2)}) copy-start(bf16[2,4096,192]{1,2,0:T(8,128)(2,1)} %param.28) | copy-start | bytes 9437188
  128.4 205.4 %all-gather.7.cloned.1.call-start = ((), (), s32[]{:S(2)}) async-start(), calls=%async_computation.4 | async-start | bytes 3932160 | tf_op jit(solution)/shard_map/all_gather | solution.py:361
  240.9 25.9 %copy-start.2 = (bf16[4,2,192,1024]{3,2,1,0:T(8,128)(2,1)S(1)}, bf16[4,2,192,1024]{3,2,1,0:T(8,128)(2,1)}, u32[]{:S(2)}) copy-start(bf16[4,2,192,1024]{3,2,1,0:T(8,128)(2,1)} %get-tuple-element.11) | copy-start | bytes 9437188
  342.3 7.6 %copy-start.3 = (s32[128,8]{0,1:T(8,128)S(1)}, s32[128,8]{0,1:T(8,128)}, u32[]{:S(2)}) copy-start(s32[128,8]{0,1:T(8,128)} %param.25) | copy-start | bytes 12292
  342.3 62.2 %all-to-all-start.2 = ((bf16[32,64,1024]{2,1,0:T(8,128)(2,1)}), bf16[32,64,1024]{2,1,0:T(8,128)(2,1)}, u32[]{:S(2)}, u32[]{:S(2)}) async-start(bf16[32,64,1024]{2,1,0:T(8,128)(2,1)} %down.1), calls=%async_computation.2 | async-start | bytes 8388608 | tf_op jit(solution)/shard_map/all_to_all | solution.py:363
Sparse Core Ops, SparseCore 0:
  128.5 112.3 all-gather.4
  267.0 66.4 all-gather.6

commit v2 on v1

--- a/solution.py
+++ b/solution.py
@@ -32,24 +32,20 @@
     )
 
 
+def cost(flops, size):
+    return pl.CostEstimate(flops=int(flops), bytes_accessed=int(size), transcendentals=0)
+
+
 def attend_kernel(
-    count_ref, len_ref, q_ref, nk_ref, nv_ref, ck_ref, cv_ref, proj_hbm, down_hbm,
-    out_ref, down_out, attended, proj, sem, down_sem,
+    at_ref, count_ref, len_ref, q_ref, nk_ref, nv_ref, ck_ref, cv_ref, proj_hbm, *rest, parts
 ):
-    parts = out_ref.shape[0]
-    width = out_ref.shape[2]
+    out_refs = rest[:parts]
+    attended, proj, sem = rest[parts:]
+    width = out_refs[0].shape[1]
     heads = q_ref.shape[1] // HD
     convs, depth = ck_ref.shape[0], ck_ref.shape[1]
     fetch = pltpu.make_async_copy(proj_hbm, proj, sem)
     fetch.start()
-    regroup = [
-        pltpu.make_async_copy(
-            down_hbm.at[:, :, pl.ds(j * width, width)], down_out.at[j], down_sem.at[j]
-        )
-        for j in range(parts)
-    ]
-    for copy in regroup:
-        copy.start()
     ends = []
     total = jnp.int32(0)
     for c in range(convs):
@@ -102,33 +98,28 @@
             ]
     fetch.wait()
     for j in range(parts):
-        out_ref[j] = dot(attended[...], proj[:, j * width : (j + 1) * width]).astype(bf16)
-    for copy in regroup:
-        copy.wait()
-
-
-def attend(queries, new_keys, new_values, cache_keys, cache_values, new_count, cached_len, out_proj, w_down, parts):
+        to = pl.multiple_of(lax.rem(at_ref[0] + j, parts) * width, width)
+        out_refs[j][...] = dot(attended[...], proj[:, pl.ds(to, width)]).astype(bf16)
+
+
+def attend(at, queries, new_keys, new_values, cache_keys, cache_values, new_count, cached_len, out_proj, parts):
     width = D // parts
     vmem = pl.BlockSpec(memory_space=pltpu.VMEM)
     smem = pl.BlockSpec(memory_space=pltpu.SMEM)
     hbm = pl.BlockSpec(memory_space=pl.ANY)
     return pl.pallas_call(
-        attend_kernel,
-        out_shape=(
-            jax.ShapeDtypeStruct((parts, TOK, width), bf16),
-            jax.ShapeDtypeStruct((parts,) + w_down.shape[:2] + (width,), bf16),
-        ),
-        in_specs=[smem, smem, vmem, vmem, vmem, vmem, vmem, hbm, hbm],
-        out_specs=(vmem, hbm),
+        functools.partial(attend_kernel, parts=parts),
+        out_shape=[jax.ShapeDtypeStruct((TOK, width), bf16)] * parts,
+        in_specs=[smem, smem, smem, vmem, vmem, vmem, vmem, vmem, hbm],
+        out_specs=[vmem] * parts,
         scratch_shapes=[
             pltpu.VMEM((TOK, queries.shape[1]), bf16),
             pltpu.VMEM(out_proj.shape, bf16),
             pltpu.SemaphoreType.DMA,
-            pltpu.SemaphoreType.DMA((parts,)),
         ],
         compiler_params=params(),
         name="attend",
-    )(new_count, cached_len, queries, new_keys, new_values, cache_keys, cache_values, out_proj, w_down)
+    )(at, new_count, cached_len, queries, new_keys, new_values, cache_keys, cache_values, out_proj)
 
 
 def thirds(v):
@@ -137,10 +128,12 @@
     return high, mid, v - high - mid
 
 
-def prepare_kernel(at_ref, terms_ref, residual_ref, gain_ref, ids_ref, gate_ref, payload_ref, stream_ref):
-    del at_ref
+def prepare_kernel(at_ref, *refs, parts):
+    terms_refs = refs[:parts]
+    residual_ref, gain_ref, ids_ref, gate_ref, payload_ref, stream_ref, at_out = refs[parts:]
+    at_out[0] = at_ref[0]
     total = residual_ref[...].astype(f32)
-    terms = sum(terms_ref[j].astype(f32) for j in range(terms_ref.shape[0]))
+    terms = sum(ref[...].astype(f32) for ref in terms_refs)
     stream = (total + terms).astype(bf16)
     stream_ref[...] = stream
     s = stream.astype(f32)
@@ -164,18 +157,20 @@
 
 
 def prepare(at, terms, residual, gain, ids_t, gate_t):
-    width = terms.shape[2]
-    return pl.pallas_call(
-        prepare_kernel,
+    parts = len(terms)
+    width = terms[0].shape[1]
+    return pl.pallas_call(
+        functools.partial(prepare_kernel, parts=parts),
         out_shape=(
             jax.ShapeDtypeStruct((TOK + META, width), bf16),
             jax.ShapeDtypeStruct((TOK, width), bf16),
+            jax.ShapeDtypeStruct((1,), jnp.int32),
         ),
         grid_spec=pltpu.PrefetchScalarGridSpec(
             num_scalar_prefetch=1,
             grid=(1,),
-            in_specs=[
-                pl.BlockSpec(terms.shape, lambda i, at: (0, 0, 0)),
+            in_specs=[pl.BlockSpec((TOK, width), lambda i, at: (0, 0))] * parts
+            + [
                 pl.BlockSpec((TOK, width), lambda i, at: (0, at[0])),
                 pl.BlockSpec((1, width), lambda i, at: (0, at[0])),
                 pl.BlockSpec(ids_t.shape, lambda i, at: (0, 0)),
@@ -184,25 +179,28 @@
             out_specs=[
                 pl.BlockSpec((TOK + META, width), lambda i, at: (0, 0)),
                 pl.BlockSpec((TOK, width), lambda i, at: (0, 0)),
+                pl.BlockSpec(memory_space=pltpu.SMEM),
             ],
         ),
         compiler_params=params("arbitrary"),
         name="prepare",
-    )(at, terms, residual, gain, ids_t, gate_t)
-
-
-def experts_kernel(first_ref, x_ref, gate_w_ref, up_w_ref, act_ref, rows, groups, parts):
+    )(at, *terms, residual, gain, ids_t, gate_t)
+
+
+def experts_kernel(first_ref, x_ref, gate_w_ref, up_w_ref, *refs, groups, parts, held):
+    act_ref, rows = refs[held:]
     width = x_ref.shape[2]
     topk = width // TOK
     local = gate_w_ref.shape[0]
-    hidden = gate_w_ref.shape[2]
+    pair = 2
     earlier = (
         lax.broadcasted_iota(jnp.int32, (TOK, TOK), 0)
         < lax.broadcasted_iota(jnp.int32, (TOK, TOK), 1)
     ).astype(bf16)
     slots = lax.broadcasted_iota(jnp.int32, (CAP, TOK), 0).astype(f32)
-    scales = [[], []]
-    gates = [[], []]
+    scales = [[] for _ in range(local)]
+    gates = [[] for _ in range(local)]
+    picks = [[] for _ in range(local)]
     for g in range(groups):
         meta = x_ref[g * parts, TOK:].astype(f32)
         square = jnp.zeros((1, TOK), f32)
@@ -221,18 +219,26 @@
             weights.append(sum(weight[:, k * TOK : (k + 1) * TOK] for k in range(topk)))
         named = jnp.concatenate(members + [jnp.zeros((8 - local, TOK), f32)], axis=0)
         slot = dot(named.astype(bf16), earlier)
-        picks = []
         for e in range(local):
             pick = (slots == slot[e : e + 1]) & (members[e] > 0.5)
-            picks.append(jnp.where(pick, 1.0, 0.0))
+            picks[e].append(jnp.where(pick, 1.0, 0.0))
             scales[e].append(jnp.sum(jnp.where(pick, scale, 0.0), axis=1, keepdims=True))
             gates[e].append(jnp.sum(jnp.where(pick, weights[e], 0.0), axis=1, keepdims=True))
-        picks = jnp.concatenate(picks, axis=0).astype(bf16)
+    size = pair * CAP
+    blank = jnp.zeros((CAP, TOK), f32)
+    for g in range(0, groups, pair):
+        lines = []
+        for e in range(local):
+            for i in range(pair):
+                line = [picks[e][g + i] if j == i else blank for j in range(pair)]
+                lines.append(jnp.concatenate(line, axis=1))
+        pick = jnp.concatenate(lines, axis=0).astype(bf16)
         for q in range(parts):
-            picked = dot(picks, x_ref[g * parts + q, :TOK]).astype(bf16)
+            x = jnp.concatenate([x_ref[(g + i) * parts + q, :TOK] for i in range(pair)], axis=0)
+            picked = dot(pick, x).astype(bf16)
             for e in range(local):
-                rows[e, g * CAP : (g + 1) * CAP, q * width : (q + 1) * width] = picked[
-                    e * CAP : (e + 1) * CAP
+                rows[e, g * CAP : g * CAP + size, q * width : (q + 1) * width] = picked[
+                    e * size : (e + 1) * size
                 ]
     done = []
     for e in range(local):
@@ -244,58 +250,66 @@
     act_ref[...] = jnp.concatenate(done, axis=1)
 
 
-def run_experts(first, gathered, w_gate, w_up, parts):
+def run_experts(first, gathered, w_gate, w_up, held, parts, chunk, chunks):
     groups = 4
-    total = gathered.shape[0] // parts
+    steps = gathered.shape[0] // parts // groups // chunks
     local, _, hidden = w_gate.shape
     whole = pl.BlockSpec(w_gate.shape, lambda i: (0, 0, 0), pipeline_mode=pl.Buffered(1))
     return pl.pallas_call(
-        functools.partial(experts_kernel, groups=groups, parts=parts),
-        out_shape=jax.ShapeDtypeStruct((total * CAP, local * hidden), bf16),
-        grid=(total // groups,),
+        functools.partial(experts_kernel, groups=groups, parts=parts, held=len(held)),
+        out_shape=jax.ShapeDtypeStruct((steps * groups * CAP, local * hidden), bf16),
+        grid=(steps,),
         in_specs=[
             pl.BlockSpec(memory_space=pltpu.SMEM),
-            pl.BlockSpec((groups * parts,) + gathered.shape[1:], lambda i: (i, 0, 0)),
+            pl.BlockSpec((groups * parts,) + gathered.shape[1:], lambda i: (chunk * steps + i, 0, 0)),
             whole,
             whole,
-        ],
+        ]
+        + [pl.BlockSpec(memory_space=pl.ANY)] * len(held),
         out_specs=pl.BlockSpec((groups * CAP, local * hidden), lambda i: (i, 0)),
         scratch_shapes=[pltpu.VMEM((local, groups * CAP, D), bf16)],
         compiler_params=params("arbitrary"),
+        cost_estimate=cost(7e9, gathered.size) if chunk == 0 else cost(1, 1),
         name="experts",
-    )(first, gathered, w_gate, w_up)
-
-
-def down_kernel(act_ref, w_ref, out_ref):
-    parts, local, hidden, width = w_ref.shape
+    )(first, gathered, w_gate, w_up, *held)
+
+
+def down_kernel(*refs, parts):
+    act_refs, w_refs, out_ref = refs[:parts], refs[parts : 2 * parts], refs[-1]
+    local, hidden, width = w_refs[0].shape
     groups = out_ref.shape[0]
     for e in range(local):
         total = sum(
-            dot(act_ref[q, :, e * hidden : (e + 1) * hidden], w_ref[q, e]) for q in range(parts)
+            dot(act_refs[q][:, e * hidden : (e + 1) * hidden], w_refs[q][e]) for q in range(parts)
         )
         out_ref[:, e * CAP : (e + 1) * CAP] = total.astype(bf16).reshape(groups, CAP, width)
 
 
-def run_down(act, w):
-    parts, local, hidden, width = w.shape
+def run_down(acts, ws, chunk, chunks, filled):
+    local, hidden, width = ws[0].shape
     groups = 8
-    total = act.shape[1] // CAP
-    return pl.pallas_call(
-        down_kernel,
+    held = [] if filled is None else [filled]
+    total = acts[0].shape[0] // CAP * chunks
+    steps = total // groups // chunks
+    return pl.pallas_call(
+        functools.partial(down_kernel, parts=len(acts)),
         out_shape=jax.ShapeDtypeStruct((total, local * CAP, width), bf16),
-        grid=(total // groups,),
-        in_specs=[
-            pl.BlockSpec((parts, groups * CAP, act.shape[2]), lambda i: (0, i, 0)),
-            pl.BlockSpec(w.shape, lambda i: (0, 0, 0, 0), pipeline_mode=pl.Buffered(1)),
-        ],
-        out_specs=pl.BlockSpec((groups, local * CAP, width), lambda i: (i, 0, 0)),
+        grid=(steps,),
+        in_specs=[pl.BlockSpec((groups * CAP, local * hidden), lambda i: (i, 0))] * len(acts)
+        + [pl.BlockSpec(ws[0].shape, lambda i: (0, 0, 0), pipeline_mode=pl.Buffered(1))] * len(ws)
+        + [pl.BlockSpec(memory_space=pl.ANY)] * len(held),
+        out_specs=pl.BlockSpec(
+            (groups, local * CAP, width), lambda i: (chunk * steps + i, 0, 0)
+        ),
+        input_output_aliases={2 * len(acts): 0} if held else {},
         compiler_params=params("arbitrary"),
+        cost_estimate=cost(1, 1),
         name="down",
-    )(act, w)
-
-
-def combine_kernel(ids_ref, rows_ref, stream_ref, out_ref):
-    slots = rows_ref.shape[0]
+    )(*acts, *ws, *held)
+
+
+def place_kernel(ids_ref, picks_ref):
+    slots = picks_ref.shape[1]
     experts = slots // CAP
     ids = ids_ref[...]
     names = lax.broadcasted_iota(jnp.int32, (TOK, experts), 1)
@@ -311,20 +325,52 @@
     ).astype(bf16)
     place = dot(place.astype(bf16), spread)
     own = (lax.broadcasted_iota(jnp.int32, (TOK, slots), 1) % CAP + 1).astype(f32)
-    picks = (place == own).astype(bf16)
-    out_ref[...] = (stream_ref[...].astype(f32) + dot(picks, rows_ref[...])).astype(bf16)
-
-
-def combine(ids, rows, stream):
+    picks_ref[...] = (place == own).astype(bf16)
+
+
+def places(ids, slots):
     vmem = pl.BlockSpec(memory_space=pltpu.VMEM)
+    return pl.pallas_call(
+        place_kernel,
+        out_shape=jax.ShapeDtypeStruct((TOK, slots), bf16),
+        in_specs=[vmem],
+        out_specs=vmem,
+        compiler_params=params(),
+        cost_estimate=cost(1e8, 1e6),
+        name="places",
+    )(ids)
+
+
+def combine_kernel(picks_ref, rows_ref, stream_ref, out_ref, total):
+    @pl.when(pl.program_id(0) == 0)
+    def _():
+        total[...] = stream_ref[...].astype(f32)
+
+    total[...] += dot(picks_ref[...], rows_ref[...])
+
+    @pl.when(pl.program_id(0) == pl.num_programs(0) - 1)
+    def _():
+        out_ref[...] = total[...].astype(bf16)
+
+
+def combine(picks, rows, stream):
+    steps = 2
+    size = rows.shape[0] // steps
+    whole = pl.BlockSpec(stream.shape, lambda i: (0, 0))
     return pl.pallas_call(
         combine_kernel,
         out_shape=jax.ShapeDtypeStruct(stream.shape, bf16),
-        in_specs=[vmem] * 3,
-        out_specs=vmem,
-        compiler_params=params(),
+        grid=(steps,),
+        in_specs=[
+            pl.BlockSpec((TOK, size), lambda i: (0, i)),
+            pl.BlockSpec((size, rows.shape[1]), lambda i: (i, 0)),
+            whole,
+        ],
+        out_specs=whole,
+        scratch_shapes=[pltpu.VMEM(stream.shape, f32)],
+        compiler_params=params("arbitrary"),
         name="combine",
-    )(ids, rows, stream)
+    )(picks, rows, stream)
 
 
 def on_device(
@@ -347,21 +393,43 @@
     parts = lax.axis_size("tp")
     at = lax.axis_index("tp").astype(jnp.int32).reshape(1)
     first = (lax.axis_index("ep") * w_gate.shape[0]).astype(jnp.int32).reshape(1)
-    terms, down_parts = attend(
-        queries, new_keys, new_values, cache_keys, cache_values, new_count, cached_len,
-        out_proj, w_down, parts,
-    )
-    terms = lax.all_to_all(terms, "tp", split_axis=0, concat_axis=0, tiled=True)
-    down_w = lax.all_to_all(down_parts, "tp", split_axis=0, concat_axis=0, tiled=True)
-    payload, stream = prepare(
+    local = w_gate.shape[0]
+    width = D // parts
+
+    def shift(v, by):
+        return lax.ppermute(v, "tp", [(i, (i + by) % parts) for i in range(parts)])
+
+    def spread(vs):
+        return [vs[0]] + [shift(vs[j], j) for j in range(1, parts)]
+
+    terms = spread(
+        attend(
+            at, queries, new_keys, new_values, cache_keys, cache_values, new_count, cached_len,
+            out_proj, parts,
+        )
+    )
+    payload, stream, at = prepare(
         at, terms, residual, norm_gain.reshape(1, D), expert_ids.T, gate_scale.T
     )
     gathered = lax.all_gather(payload, ("ep", "tp"))
-    act = run_experts(first, gathered, w_gate, w_up, parts)
-    act = lax.all_gather(act, "tp")
-    rows = run_down(act, down_w)
+    down_w = spread(
+        [
+            lax.dynamic_slice_in_dim(w_down, lax.rem(at[0] + j, parts) * width, width, 2)
+            for j in range(parts)
+        ]
+    )
+    picks = places(expert_ids, lax.axis_size("ep") * local * CAP)
+    chunks = 2
+    held = [*down_w, picks]
+    acts = []
+    for chunk in range(chunks):
+        acts.append(run_experts(first, gathered, w_gate, w_up, held, parts, chunk, chunks))
+        held = acts[-1:]
+    rows = None
+    for chunk, act in enumerate(acts):
+        rows = run_down(spread([act] * parts), down_w, chunk, chunks, rows)
     rows = lax.all_to_all(rows, "ep", split_axis=0, concat_axis=0, tiled=True)
-    return combine(expert_ids, rows.reshape(-1, rows.shape[2]), stream)
+    return combine(picks, rows.reshape(-1, width), stream)
 
 
 def solution(mesh):

time: 416 us -> 294 us (0.71)
  Pallas kernels: 140 us -> 58.1 us
  waiting for transfers between devices: 171 us -> 123 us
  blocking collectives: 67 us -> 56.2 us
  starting transfers between devices: 12 us -> 18.1 us
  local copies, waits for them, and re-layouts: 12.6 us -> 17.6 us
    pallas_call x3 -> x5, Pallas kernels: 110 us -> 26.3 us  [the longest x2 11.5 us: run_down(): pl.pallas_call(functools.partial(down_kernel, parts=len(acts)), out_shape...]
    all_to_all x2 -> x0, waiting for transfers between devices: 68.3 us -> none  [the longest x1 53.8 us: on_device(): rows = lax.all_to_all(rows, 'ep', split_axis=0, concat_axis=0, tiled=True)]
    ppermute x0 -> x12, waiting for transfers between devices: none -> 53.4 us  [shift(): return lax.ppermute(v, 'tp', [(i, (i + by) % parts) for i in range(parts)])]
    all_gather x1, waiting for transfers between devices: 102 us -> 69.4 us  [on_device(): gathered = lax.all_gather(payload, ('ep', 'tp'))]
    ppermute x0 -> x12, starting transfers between devices: none -> 18.1 us  [shift(): return lax.ppermute(v, 'tp', [(i, (i + by) % parts) for i in range(parts)])]
    all_to_all x2 -> x0, starting transfers between devices: 11.9 us -> none  [the longest x1 7.63 us: on_device(): rows = lax.all_to_all(rows, 'ep', split_axis=0, concat_axis=0, tiled=True)]
    all_to_all x1, blocking collectives: 67 us -> 56.2 us  [on_device(): rows = lax.all_to_all(rows, 'ep', split_axis=0, concat_axis=0, tiled=True)]
    unnamed x13 -> x33, local copies, waits for them, and re-layouts: 11.9 us -> 15.2 us
  transfers between devices with their start and end apart: 4 -> 13, of which waited for: 3 -> 9; matrix products, arithmetic and copies ran while one was open for 3% -> 5% of each run, Pallas kernels for 0% -> 8%
where the time goes in v2:
time: 294 us; the launch traced here: 290 us
  waiting for transfers between devices  123 us (42%)
  Pallas kernels  58.1 us (20%)
  blocking collectives  56.2 us (19%)
  starting transfers between devices  18.1 us (6%)
  local copies, waits for them, and re-layouts  17.6 us (6%)
  between operations  17.2 us (6%)
    all_gather x1, waiting for transfers between devices, on_device(): gathered = lax.all_gather(payload, ('ep', 'tp'))  69.4 us
    all_to_all x1, blocking collectives, on_device(): rows = lax.all_to_all(rows, 'ep', split_axis=0, concat_axis=0, tiled=True)  56.2 us
    ppermute x12, waiting for transfers between devices, shift(): return lax.ppermute(v, 'tp', [(i, (i + by) % parts) for i in range(parts)])  53.4 us
    pallas_call x2, Pallas kernels, run_experts(): pl.pallas_call(functools.partial(experts_kernel, groups=groups, parts=par...  28.1 us
    ppermute x12, starting transfers between devices, shift(): return lax.ppermute(v, 'tp', [(i, (i + by) % parts) for i in range(parts)])  18.1 us
    unnamed x33, local copies, waits for them, and re-layouts  15.2 us
    pallas_call x2, Pallas kernels, run_down(): pl.pallas_call(functools.partial(down_kernel, parts=len(acts)), out_shape...  11.5 us
    pallas_call x1, Pallas kernels, attend(): pl.pallas_call(functools.partial(attend_kernel, parts=parts), out_shape=[...  10.1 us
  transfers between devices with their start and end apart: 13, of which 9 were waited for; matrix products, arithmetic and copies ran while one was open for 5% of the time, Pallas kernels for 8%

profile of v2, /device:TPU:32, one launch (start us, length us, event | category | flops | bytes accessed | tf_op | source)
XLA Modules:
  0.0 290.0 jit_solution(7121674428335817500)
XLA Ops:
  6.5 10.1 %attend.1 = (bf16[128,1024]{1,0:T(8,128)(2,1)}, bf16[128,1024]{1,0:T(8,128)(2,1)}, bf16[128,1024]{1,0:T(8,128)(2,1)}, bf16[128,1024]{1,0:T(8,128)(2,1)}) custom-call(s32[1]{0:T(128)} %bitcast.1.at_ref, s32[4]{0:T(128)} %count_ref.1, s32[4]{0:T(128)} %len_ref.1, bf16[128,1024]{1,0:T(8,128)(2,1)} %q_ref.1, bf16[128,128]{1,0:T(8,128)(2,1)} %nk_ref.1, ...), custom_call_target="tpu_custom_call" | custom-call | tf_op jit(solution)/shard_map/attend/pallas_call | solution.py:110
  16.7 1.6 collective-permute-start
  18.2 2.7 collective-permute-start.1
  21.0 1.4 collective-permute-start.2
  22.4 0.6 reshape.14.refs_5_
  23.0 3.3 %collective-permute-done.refs_1_ = bf16[128,1024]{1,0:T(8,128)(2,1)S(1)} collective-permute-done((bf16[128,1024]{1,0:T(8,128)(2,1)}, bf16[128,1024]{1,0:T(8,128)(2,1)S(1)}, u32[]{:S(2)}, u32[]{:S(2)}) %collective-permute-start) | collective-permute-done | bytes 262176 | tf_op jit(solution)/shard_map/ppermute | solution.py:400
  26.4 6.4 %collective-permute-done.1.refs_2_ = bf16[128,1024]{1,0:T(8,128)(2,1)S(1)} collective-permute-done((bf16[128,1024]{1,0:T(8,128)(2,1)}, bf16[128,1024]{1,0:T(8,128)(2,1)S(1)}, u32[]{:S(2)}, u32[]{:S(2)}) %collective-permute-start.1) | collective-permute-done | bytes 262176 | tf_op jit(solution)/shard_map/ppermute | solution.py:400
  32.8 0.0 collective-permute-done.2.refs_3_
  32.8 0.7 copy-done.11
  33.5 0.1 copy-done.12
  33.6 2.4 prepare.1
  36.0 0.0 all-gather.3.cloned.1.call-update
  39.8 1.7 constant_dynamic-slice_fusion
  41.5 2.2 collective-permute-start.5
  43.6 0.0 collective-permute-start.3
  43.7 2.4 collective-permute-start.4
  46.1 0.0 copy-done.13
  46.1 0.7 copy.17.ids_ref
  46.8 6.1 %copy.20.gate_w_ref = bf16[2,4096,192]{2,1,0:T(8,128)(2,1)} copy(bf16[2,4096,192]{1,2,0:T(8,128)(2,1)} %param.27) | data formatting | bytes 6291456 | tf_op args[12]
  52.9 6.1 %copy.21.up_w_ref = bf16[2,4096,192]{2,1,0:T(8,128)(2,1)} copy(bf16[2,4096,192]{1,2,0:T(8,128)(2,1)} %param.28) | data formatting | bytes 6291456 | tf_op args[13]
  59.0 2.3 places.1.refs_4_.picks_ref
  61.3 18.8 %collective-permute-done.5.refs_3_.refs_7_ = bf16[2,192,1024]{2,1,0:T(8,128)(2,1)S(1)} collective-permute-done((bf16[2,192,1024]{2,1,0:T(8,128)(2,1)}, bf16[2,192,1024]{2,1,0:T(8,128)(2,1)S(1)}, u32[]{:S(2)}, u32[]{:S(2)}) %collective-permute-start.5) | collective-permute-done | bytes 786464 | tf_op jit(solution)/shard_map/ppermute | solution.py:400
  80.1 2.8 collective-permute-done.3.refs_1_.refs_5_
  82.8 9.9 %collective-permute-done.4.refs_2_.refs_6_ = bf16[2,192,1024]{2,1,0:T(8,128)(2,1)S(1)} collective-permute-done((bf16[2,192,1024]{2,1,0:T(8,128)(2,1)}, bf16[2,192,1024]{2,1,0:T(8,128)(2,1)S(1)}, u32[]{:S(2)}, u32[]{:S(2)}) %collective-permute-start.4) | collective-permute-done | bytes 786464 | tf_op jit(solution)/shard_map/ppermute | solution.py:400
  92.7 69.4 %all-gather.3.cloned.1.call-done = bf16[18432,1024]{1,0:T(8,128)(2,1)} async-done(((bf16[144,1024]{1,0:T(8,128)(2,1)}), bf16[18432,1024]{1,0:T(8,128)(2,1)}) %all-gather.3.cloned.1.call-update) | async-done | bytes 37748752 | tf_op jit(solution)/shard_map/all_gather | solution.py:414
  162.1 0.0 copy-done
  162.1 0.0 copy-done.2
  162.1 14.0 %experts.2.refs_0_ = bf16[512,384]{1,0:T(8,128)(2,1)} custom-call(s32[1]{0:T(128)} %bitcast.first_ref, bf16[128,144,1024]{2,1,0:T(8,128)(2,1)} %bitcast.7, bf16[2,4096,192]{2,1,0:T(8,128)(2,1)} %copy.20.gate_w_ref, bf16[2,4096,192]{2,1,0:T(8,128)(2,1)} %copy.21.up_w_ref, bf16[2,192,1024]{2,1,0:T(8,128)(2,1)} %get-tuple-element.21.refs_0_.refs_4_, ...), custom_call_target="tpu_custom_call" | custom-call | flops 7000000000 | bytes 18874368 | tf_op jit(solution)/shard_map/experts/pallas_call | solution.py:258
  176.2 2.2 collective-permute-start.11
  178.4 0.8 collective-permute-start.10
  179.2 0.9 collective-permute-start.9
  180.1 14.0 %experts.3.refs_0_ = bf16[512,384]{1,0:T(8,128)(2,1)} custom-call(s32[1]{0:T(128)} %bitcast.first_ref, bf16[128,144,1024]{2,1,0:T(8,128)(2,1)} %bitcast.8, bf16[2,4096,192]{2,1,0:T(8,128)(2,1)} %copy.20.gate_w_ref, bf16[2,4096,192]{2,1,0:T(8,128)(2,1)} %copy.21.up_w_ref, bf16[512,384]{1,0:T(8,128)(2,1)} %experts.2.refs_0_), custom_call_target="tpu_custom_call" | custom-call | flops 1 | bytes 1 | tf_op jit(solution)/shard_map/experts/pallas_call | solution.py:258
  194.1 2.4 collective-permute-start.8
  196.5 1.5 collective-permute-start.7
  198.0 0.0 collective-permute-done.11.refs_3_
  198.0 0.0 collective-permute-start.6
  198.0 0.0 collective-permute-done.10.refs_2_
  198.0 0.0 copy-start.7
  198.0 1.5 collective-permute-done.9.refs_1_
  199.5 0.8 copy-done.8
  200.3 5.8 %down.2.refs_8_ = bf16[32,64,1024]{2,1,0:T(8,128)(2,1)} custom-call(bf16[512,384]{1,0:T(8,128)(2,1)} %experts.2.refs_0_, bf16[512,384]{1,0:T(8,128)(2,1)} %copy-done.8, bf16[512,384]{1,0:T(8,128)(2,1)} %copy-done.7, bf16[512,384]{1,0:T(8,128)(2,1)} %copy-done.5, bf16[2,192,1024]{2,1,0:T(8,128)(2,1)} %get-tuple-element.21.refs_0_.refs_4_, ...), custom_call_target="tpu_custom_call" | custom-call | flops 1 | bytes 1 | tf_op jit(solution)/shard_map/down/pallas_call | solution.py:294
  206.1 7.2 %collective-permute-done.8.refs_3_ = bf16[512,384]{1,0:T(8,128)(2,1)S(1)} collective-permute-done((bf16[512,384]{1,0:T(8,128)(2,1)}, bf16[512,384]{1,0:T(8,128)(2,1)S(1)}, u32[]{:S(2)}, u32[]{:S(2)}) %collective-permute-start.8) | collective-permute-done | bytes 393248 | tf_op jit(solution)/shard_map/ppermute | solution.py:400
  213.3 0.0 collective-permute-done.7.refs_2_
  213.3 3.6 %collective-permute-done.6.refs_1_ = bf16[512,384]{1,0:T(8,128)(2,1)S(1)} collective-permute-done((bf16[512,384]{1,0:T(8,128)(2,1)}, bf16[512,384]{1,0:T(8,128)(2,1)S(1)}, u32[]{:S(2)}, u32[]{:S(2)}) %collective-permute-start.6) | collective-permute-done | bytes 393248 | tf_op jit(solution)/shard_map/ppermute | solution.py:400
  216.8 0.8 copy-done.9
  217.6 5.8 %down.3 = bf16[32,64,1024]{2,1,0:T(8,128)(2,1)} custom-call(bf16[512,384]{1,0:T(8,128)(2,1)} %experts.3.refs_0_, bf16[512,384]{1,0:T(8,128)(2,1)} %copy-done.9, bf16[512,384]{1,0:T(8,128)(2,1)} %copy-done.6, bf16[512,384]{1,0:T(8,128)(2,1)} %copy-done.4, bf16[2,192,1024]{2,1,0:T(8,128)(2,1)} %get-tuple-element.21.refs_0_.refs_4_, ...), custom_call_target="tpu_custom_call", output_to_operand_aliasing={{}: (8, {})} | custom-call | flops 1 | bytes 1 | tf_op jit(solution)/shard_map/down/pallas_call | solution.py:294
  223.4 56.2 %all_to_all.5 = bf16[32,64,1024]{2,1,0:T(8,128)(2,1)} all-to-all(bf16[32,64,1024]{2,1,0:T(8,128)(2,1)} %down.3), channel_id=1, replica_groups=mesh['ep'=32,'tp'=4] {'ep'}, dimensions={0} | all-to-all | bytes 8388608 | tf_op jit(solution)/shard_map/all_to_all | solution.py:431
  279.5 3.7 %combine.1 = bf16[128,1024]{1,0:T(8,128)(2,1)} custom-call(bf16[128,2048]{1,0:T(8,128)(2,1)} %places.1.refs_4_.picks_ref, bf16[2048,1024]{1,0:T(8,128)(2,1)} %bitcast.9, bf16[128,1024]{1,0:T(8,128)(2,1)} %get-tuple-element.18.stream_ref), custom_call_target="tpu_custom_call" | custom-call | tf_op jit(solution)/shard_map/combine/pallas_call | solution.py:360
  (23 shorter events, 0.0 us)
Async XLA Ops:
  6.5 155.6 %all-gather.3.cloned.1.call-start = ((), (), s32[]{:S(2)}) async-start(), calls=%async_computation.1 | async-start | bytes 38043648 | tf_op jit(solution)/shard_map/all_gather | solution.py:414
  6.5 15.9 %copy-start.14 = (bf16[4096]{0:T(1024)(128)(2,1)S(1)}, bf16[4096]{0:T(1024)(128)(2,1)}, u32[]{:S(2)}) copy-start(bf16[4096]{0:T(1024)(128)(2,1)} %param.24) | copy-start | bytes 24580
  6.5 33.2 %copy-start.3 = (bf16[2,192,4096]{2,1,0:T(8,128)(2,1)S(1)}, bf16[2,192,4096]{2,1,0:T(8,128)(2,1)}, u32[]{:S(2)}) copy-start(bf16[2,192,4096]{2,1,0:T(8,128)(2,1)} %param.29) | copy-start | bytes 9437188
  16.7 9.7 %collective-permute-start = (bf16[128,1024]{1,0:T(8,128)(2,1)}, bf16[128,1024]{1,0:T(8,128)(2,1)S(1)}, u32[]{:S(2)}, u32[]{:S(2)}) collective-permute-start(bf16[128,1024]{1,0:T(8,128)(2,1)} %get-tuple-element.13), channel_id=1, source_target_pairs={{0,1},{1,2},{2,3},{3,0},{4,5},{5,6},{6,7},{7,4},{8,9},{9,10},{10,1... | collective-permute-start | bytes 786440 | tf_op jit(solution)/shard_map/ppermute | solution.py:400
  18.2 14.6 %collective-permute-start.1 = (bf16[128,1024]{1,0:T(8,128)(2,1)}, bf16[128,1024]{1,0:T(8,128)(2,1)S(1)}, u32[]{:S(2)}, u32[]{:S(2)}) collective-permute-start(bf16[128,1024]{1,0:T(8,128)(2,1)} %get-tuple-element.14), channel_id=1, source_target_pairs={{0,2},{1,3},{2,0},{3,1},{4,6},{5,7},{6,4},{7,5},{8,10},{9,11},{10,... | collective-permute-start | bytes 786440 | tf_op jit(solution)/shard_map/ppermute | solution.py:400
  21.0 11.8 %collective-permute-start.2 = (bf16[128,1024]{1,0:T(8,128)(2,1)}, bf16[128,1024]{1,0:T(8,128)(2,1)S(1)}, u32[]{:S(2)}, u32[]{:S(2)}) collective-permute-start(bf16[128,1024]{1,0:T(8,128)(2,1)} %get-tuple-element.15), channel_id=1, source_target_pairs={{0,3},{1,0},{2,1},{3,2},{4,7},{5,4},{6,5},{7,6},{8,11},{9,8},{10,9... | collective-permute-start | bytes 786440 | tf_op jit(solution)/shard_map/ppermute | solution.py:400
  26.4 6.4 %copy-start.10 = (bf16[128,1024]{1,0:T(8,128)(2,1)}, bf16[128,1024]{1,0:T(8,128)(2,1)S(1)}, u32[]{:S(2)}) copy-start(bf16[128,1024]{1,0:T(8,128)(2,1)S(1)} %collective-permute-done.refs_1_) | copy-start | bytes 786436
  32.8 0.7 copy-start.11
  32.8 0.8 copy-start.12
  33.6 12.5 %copy-start.13 = (s32[128,8]{0,1:T(8,128)S(1)}, s32[128,8]{0,1:T(8,128)}, u32[]{:S(2)}) copy-start(s32[128,8]{0,1:T(8,128)} %param.25) | copy-start | bytes 12292
  41.5 38.6 %collective-permute-start.5 = (bf16[2,192,1024]{2,1,0:T(8,128)(2,1)}, bf16[2,192,1024]{2,1,0:T(8,128)(2,1)S(1)}, u32[]{:S(2)}, u32[]{:S(2)}) collective-permute-start(bf16[2,192,1024]{2,1,0:T(8,128)(2,1)} %get-tuple-element.19), channel_id=1, source_target_pairs={{0,3},{1,0},{2,1},{3,2},{4,7},{5,4},{6,5},{7,6},{8,11},{9,8},{10,9... | collective-permute-start | bytes 2359304 | tf_op jit(solution)/shard_map/ppermute | solution.py:400
  43.6 39.2 %collective-permute-start.3 = (bf16[2,192,1024]{2,1,0:T(8,128)(2,1)}, bf16[2,192,1024]{2,1,0:T(8,128)(2,1)S(1)}, u32[]{:S(2)}, u32[]{:S(2)}) collective-permute-start(bf16[2,192,1024]{2,1,0:T(8,128)(2,1)} %get-tuple-element.20), channel_id=1, source_target_pairs={{0,1},{1,2},{2,3},{3,0},{4,5},{5,6},{6,7},{7,4},{8,9},{9,10},{10,1... | collective-permute-start | bytes 2359304 | tf_op jit(solution)/shard_map/ppermute | solution.py:400
  43.7 49.1 %collective-permute-start.4 = (bf16[2,192,1024]{2,1,0:T(8,128)(2,1)}, bf16[2,192,1024]{2,1,0:T(8,128)(2,1)S(1)}, u32[]{:S(2)}, u32[]{:S(2)}) collective-permute-start(bf16[2,192,1024]{2,1,0:T(8,128)(2,1)} %get-tuple-element.22), channel_id=1, source_target_pairs={{0,2},{1,3},{2,0},{3,1},{4,6},{5,7},{6,4},{7,5},{8,10},{9,11},{10,... | collective-permute-start | bytes 2359304 | tf_op jit(solution)/shard_map/ppermute | solution.py:400
  80.0 82.1 %copy-start = (bf16[2,192,1024]{2,1,0:T(8,128)(2,1)}, bf16[2,192,1024]{2,1,0:T(8,128)(2,1)S(1)}, u32[]{:S(2)}) copy-start(bf16[2,192,1024]{2,1,0:T(8,128)(2,1)S(1)} %collective-permute-done.5.refs_3_.refs_7_) | copy-start | bytes 2359300
  82.8 79.3 %copy-start.1 = (bf16[2,192,1024]{2,1,0:T(8,128)(2,1)}, bf16[2,192,1024]{2,1,0:T(8,128)(2,1)S(1)}, u32[]{:S(2)}) copy-start(bf16[2,192,1024]{2,1,0:T(8,128)(2,1)S(1)} %collective-permute-done.3.refs_1_.refs_5_) | copy-start | bytes 2359300
  92.7 69.4 %copy-start.2 = (bf16[2,192,1024]{2,1,0:T(8,128)(2,1)}, bf16[2,192,1024]{2,1,0:T(8,128)(2,1)S(1)}, u32[]{:S(2)}) copy-start(bf16[2,192,1024]{2,1,0:T(8,128)(2,1)S(1)} %collective-permute-done.4.refs_2_.refs_6_) | copy-start | bytes 2359300
  176.2 21.8 %collective-permute-start.11 = (bf16[512,384]{1,0:T(8,128)(2,1)}, bf16[512,384]{1,0:T(8,128)(2,1)S(1)}, u32[]{:S(2)}, u32[]{:S(2)}) collective-permute-start(bf16[512,384]{1,0:T(8,128)(2,1)} %experts.2.refs_0_), channel_id=1, source_target_pairs={{0,3},{1,0},{2,1},{3,2},{4,7},{5,4},{6,5},{7,6},{8,11},{9,8},{10,9... | collective-permute-start | bytes 1179656 | tf_op jit(solution)/shard_map/ppermute | solution.py:400
  178.4 19.6 %collective-permute-start.10 = (bf16[512,384]{1,0:T(8,128)(2,1)}, bf16[512,384]{1,0:T(8,128)(2,1)S(1)}, u32[]{:S(2)}, u32[]{:S(2)}) collective-permute-start(bf16[512,384]{1,0:T(8,128)(2,1)} %experts.2.refs_0_), channel_id=1, source_target_pairs={{0,2},{1,3},{2,0},{3,1},{4,6},{5,7},{6,4},{7,5},{8,10},{9,11},{10,... | collective-permute-start | bytes 1179656 | tf_op jit(solution)/shard_map/ppermute | solution.py:400
  179.2 20.3 %collective-permute-start.9 = (bf16[512,384]{1,0:T(8,128)(2,1)}, bf16[512,384]{1,0:T(8,128)(2,1)S(1)}, u32[]{:S(2)}, u32[]{:S(2)}) collective-permute-start(bf16[512,384]{1,0:T(8,128)(2,1)} %experts.2.refs_0_), channel_id=1, source_target_pairs={{0,1},{1,2},{2,3},{3,0},{4,5},{5,6},{6,7},{7,4},{8,9},{9,10},{10,1... | collective-permute-start | bytes 1179656 | tf_op jit(solution)/shard_map/ppermute | solution.py:400
  194.1 19.1 %collective-permute-start.8 = (bf16[512,384]{1,0:T(8,128)(2,1)}, bf16[512,384]{1,0:T(8,128)(2,1)S(1)}, u32[]{:S(2)}, u32[]{:S(2)}) collective-permute-start(bf16[512,384]{1,0:T(8,128)(2,1)} %experts.3.refs_0_), channel_id=1, source_target_pairs={{0,3},{1,0},{2,1},{3,2},{4,7},{5,4},{6,5},{7,6},{8,11},{9,8},{10,9... | collective-permute-start | bytes 1179656 | tf_op jit(solution)/shard_map/ppermute | solution.py:400
  196.5 16.7 %collective-permute-start.7 = (bf16[512,384]{1,0:T(8,128)(2,1)}, bf16[512,384]{1,0:T(8,128)(2,1)S(1)}, u32[]{:S(2)}, u32[]{:S(2)}) collective-permute-start(bf16[512,384]{1,0:T(8,128)(2,1)} %experts.3.refs_0_), channel_id=1, source_target_pairs={{0,2},{1,3},{2,0},{3,1},{4,6},{5,7},{6,4},{7,5},{8,10},{9,11},{10,... | collective-permute-start | bytes 1179656 | tf_op jit(solution)/shard_map/ppermute | solution.py:400
  198.0 1.5 copy-start.5
  198.0 18.8 %collective-permute-start.6 = (bf16[512,384]{1,0:T(8,128)(2,1)}, bf16[512,384]{1,0:T(8,128)(2,1)S(1)}, u32[]{:S(2)}, u32[]{:S(2)}) collective-permute-start(bf16[512,384]{1,0:T(8,128)(2,1)} %experts.3.refs_0_), channel_id=1, source_target_pairs={{0,1},{1,2},{2,3},{3,0},{4,5},{5,6},{6,7},{7,4},{8,9},{9,10},{10,1... | collective-permute-start | bytes 1179656 | tf_op jit(solution)/shard_map/ppermute | solution.py:400
  198.0 1.5 copy-start.7
  199.5 0.8 copy-start.8
  213.2 3.6 %copy-start.4 = (bf16[512,384]{1,0:T(8,128)(2,1)}, bf16[512,384]{1,0:T(8,128)(2,1)S(1)}, u32[]{:S(2)}) copy-start(bf16[512,384]{1,0:T(8,128)(2,1)S(1)} %collective-permute-done.8.refs_3_) | copy-start | bytes 1179652
  213.3 3.6 %copy-start.6 = (bf16[512,384]{1,0:T(8,128)(2,1)}, bf16[512,384]{1,0:T(8,128)(2,1)S(1)}, u32[]{:S(2)}) copy-start(bf16[512,384]{1,0:T(8,128)(2,1)S(1)} %collective-permute-done.7.refs_2_) | copy-start | bytes 1179652
  216.8 0.8 copy-start.9
Sparse Core Ops, SparseCore 0:
  36.1 125.9 all-gather.2
